TPU v7x, 32 devices: a whole 2x2x4 slice. The times are simulated.
32 devices in a mesh: leaf: 16 (over z, y, x), panel: 2 (over core).
Axes of the slice: x: 2, y: 2, z: 4, core: 2. Of those that a mesh axis runs over, the one named last changes fastest.
Arguments:
- rhs_0: bfloat16 [4096, 256], P('leaf', 'panel'), may hold values from -6 to 6
- rhs_1: bfloat16 [4096, 256], P('leaf', 'panel'), may hold values from -6 to 6
- rhs_2: bfloat16 [4096, 256], P('leaf', 'panel'), may hold values from -6 to 6
- rhs_3: bfloat16 [4096, 256], P('leaf', 'panel'), may hold values from -6 to 6
- inv_0: bfloat16 [4096, 4096], P(('leaf', 'panel')), as said below
- inv_1: bfloat16 [4096, 2048], P(('leaf', 'panel')), as said below
- inv_2: bfloat16 [4096, 1024], P(('leaf', 'panel')), as said below
- inv_3: bfloat16 [4096, 512], P(('leaf', 'panel')), as said below
- coupling_1: bfloat16 [4096, 2048], P(('leaf', 'panel')), may hold values from -0.125 to 0.125
- coupling_2: bfloat16 [4096, 1024], P(('leaf', 'panel')), may hold values from -0.1875 to 0.1875
- coupling_3: bfloat16 [4096, 512], P(('leaf', 'panel')), may hold values from -0.25 to 0.25
- update_rows_1: int32 [2, 2048], replicated, may hold values from 0 to 4095, as said below
- update_rows_2: int32 [4, 1024], replicated, may hold values from 0 to 6143, as said below
- update_rows_3: int32 [8, 512], replicated, may hold values from 0 to 7167, as said below
Outputs:
- solution_0: bfloat16 [4096, 256], P('leaf', 'panel')
- solution_1: bfloat16 [4096, 256], P('leaf', 'panel')
- solution_2: bfloat16 [4096, 256], P('leaf', 'panel')
- solution_3: bfloat16 [4096, 256], P('leaf', 'panel')
Inputs may be any that keep to these rules, and one draw needn't show every extreme that they name: `update_rows_1`: row f lists the update rows of front f of depth 1: 2048 distinct indices into its ancestor rows, holding 0 and the last ancestor row. `update_rows_2`: row f lists the update rows of front f of depth 2: 1024 distinct indices into its ancestor rows, holding 0 and the last ancestor row. `update_rows_3`: row f lists the update rows of front f of depth 3: 512 distinct indices into its ancestor rows, holding 0 and the last ancestor row. `inv_0`: the block is lower triangular with its diagonal between 0.5 and 2. `inv_1`: each 2048-row block is lower triangular with its diagonal between 0.5 and 2. `inv_2`: each 1024-row block is lower triangular with its diagonal between 0.5 and 2. `inv_3`: each 512-row block is lower triangular with its diagonal between 0.5 and 2.
All inputs are finite; a program needn't handle non-finite values.
Results may differ from a plain program's by a relative error of at most 0.014.
Values may be sent and summed in bfloat16 or wider, within the bound.
A program may use at most 64 MiB of HBM per device.

v0:
```python
import jax
import jax.numpy as jnp
from jax import lax
from jax.sharding import PartitionSpec as P

PIVOTS = 4096
LEVELS = 4


def swapped(value, axis, bit):
    mask = 2**bit
    pairs = [(source, source ^ mask) for source in range(lax.axis_size(axis))]
    return lax.ppermute(value, axis, pairs)


def double_rows(own_block, groups):
    my_index = lax.axis_index("leaf")
    for bit_pos in range(groups.bit_length() - 1):
        partner = swapped(own_block, "leaf", bit_pos)
        is_high = my_index >> bit_pos & 1 == 1
        own_block = jnp.where(
            is_high,
            jnp.concatenate([partner, own_block], axis=0),
            jnp.concatenate([own_block, partner], axis=0),
        )
    return own_block


def collect_rows(own_block, groups, front_rows):
    if groups * 4 <= lax.axis_size("leaf"):
        return double_rows(own_block, groups)
    gathered = lax.all_gather(own_block, "leaf", axis=0, tiled=True)
    row_start = lax.axis_index("leaf") // groups * front_rows
    return lax.dynamic_slice_in_dim(gathered, row_start, front_rows, 0)


def halve_sums(block, groups):
    my_index = lax.axis_index("leaf")
    for bit_pos in reversed(range(groups.bit_length() - 1)):
        half_rows = block.shape[0] // 2
        lower_half = block[:half_rows]
        upper_half = block[half_rows:]
        is_high = my_index >> bit_pos & 1 == 1
        keep_part = jnp.where(is_high, upper_half, lower_half)
        send_part = jnp.where(is_high, lower_half, upper_half)
        block = keep_part + swapped(send_part, "leaf", bit_pos)
    return block


def reduce_rows(block, groups):
    return halve_sums(block, groups)


def contract_rows(left, right):
    return lax.dot_general(
        left, right, (((0,), (0,)), ((), ())), preferred_element_type=jnp.float32
    )


def body(
    rhs_0,
    rhs_1,
    rhs_2,
    rhs_3,
    inv_0,
    inv_1,
    inv_2,
    inv_3,
    coupling_1,
    coupling_2,
    coupling_3,
    update_rows_1,
    update_rows_2,
    update_rows_3,
):
    rhs_all = [rhs_0, rhs_1, rhs_2, rhs_3]
    lists_all = [None, update_rows_1, update_rows_2, update_rows_3]
    columns = rhs_0.shape[1]
    leaf_count = lax.axis_size("leaf")
    front_sizes = [PIVOTS >> depth_now for depth_now in range(LEVELS)]
    offsets = [0]
    for depth_now in range(1, LEVELS):
        offsets.append(offsets[-1] + front_sizes[depth_now - 1])
    fetched = (
        lax.all_gather(inv_0, "panel", axis=0, tiled=True),
        lax.all_gather(inv_1, "panel", axis=0, tiled=True),
        lax.all_gather(inv_2, "panel", axis=0, tiled=True),
        lax.all_gather(inv_3, "panel", axis=0, tiled=True),
        lax.all_gather(coupling_1, "panel", axis=0, tiled=True),
        lax.all_gather(coupling_2, "panel", axis=0, tiled=True),
        lax.all_gather(coupling_3, "panel", axis=0, tiled=True),
    )
    inv_rows_all = [fetched[0], fetched[1], fetched[2], fetched[3]]
    coup_rows_all = [None, fetched[4], fetched[5], fetched[6]]
    accumulated = jnp.zeros((offsets[LEVELS - 1], columns), jnp.float32)
    forwards = [None] * LEVELS
    for depth_now in reversed(range(LEVELS)):
        groups = leaf_count >> depth_now
        front_rows = front_sizes[depth_now]
        front = lax.axis_index("leaf") // groups
        summed = rhs_all[depth_now].astype(jnp.float32)
        if depth_now < LEVELS - 1:
            summed = summed + reduce_rows(
                accumulated[offsets[depth_now] : offsets[depth_now] + front_rows], groups
            )
        combined = collect_rows(summed.astype(jnp.bfloat16), groups, front_rows)
        values = jnp.dot(
            inv_rows_all[depth_now], combined, preferred_element_type=jnp.float32
        ).astype(jnp.bfloat16)
        forwards[depth_now] = values
        if depth_now > 0:
            update = contract_rows(coup_rows_all[depth_now], values)
            row_list = lax.dynamic_index_in_dim(lists_all[depth_now], front, 0, keepdims=False)
            accumulated = accumulated.at[row_list].add(update)
    anc_values = jnp.zeros((offsets[LEVELS - 1], columns), jnp.bfloat16)
    outputs = []
    for depth_now in range(LEVELS):
        groups = leaf_count >> depth_now
        front_rows = front_sizes[depth_now]
        front = lax.axis_index("leaf") // groups
        if depth_now > 0:
            row_list = lax.dynamic_index_in_dim(lists_all[depth_now], front, 0, keepdims=False)
            picked = jnp.take(anc_values, row_list, axis=0)
            pulled = jnp.dot(coup_rows_all[depth_now], picked, preferred_element_type=jnp.float32)
            adjusted = (forwards[depth_now].astype(jnp.float32) - pulled).astype(jnp.bfloat16)
        else:
            adjusted = forwards[depth_now]
        partial_value = contract_rows(inv_rows_all[depth_now], adjusted)
        solved = reduce_rows(partial_value, groups).astype(jnp.bfloat16)
        outputs.append(solved)
        if depth_now < LEVELS - 1:
            whole_front = collect_rows(solved, groups, front_rows)
            anc_values = anc_values.at[offsets[depth_now] : offsets[depth_now] + front_rows].set(
                whole_front
            )
    return (outputs[0], outputs[1], outputs[2], outputs[3])


def solution(mesh):
    in_specs = (
        P("leaf", "panel"),
        P("leaf", "panel"),
        P("leaf", "panel"),
        P("leaf", "panel"),
        P(("leaf", "panel"), None),
        P(("leaf", "panel"), None),
        P(("leaf", "panel"), None),
        P(("leaf", "panel"), None),
        P(("leaf", "panel"), None),
        P(("leaf", "panel"), None),
        P(("leaf", "panel"), None),
        P(),
        P(),
        P(),
    )
    out_specs = (P("leaf", "panel"), P("leaf", "panel"), P("leaf", "panel"), P("leaf", "panel"))
    return jax.shard_map(body, mesh=mesh, in_specs=in_specs, out_specs=out_specs, check_vma=False)
```

profile of v0, /device:TPU:0, one launch (start us, length us, event | category | flops | bytes accessed | tf_op | source)
XLA Modules:
  0.0 579.8 jit_solution(381828962889919401)
XLA Ops:
  8.2 3.0 collective-permute-start
  11.2 2.2 all_gather.33
  14.7 2.2 all_gather.34
  17.4 4.2 scatter_custom_fusion
  24.8 6.7 %collective-permute-done.1 = f32[512,128]{0,1:T(8,128)S(1)} collective-permute-done((f32[512,128]{0,1:T(8,128)S(1)}, f32[512,128]{0,1:T(8,128)S(1)}, u32[]{:S(2)}, u32[]{:S(2)}) %collective-permute-start.1) | collective-permute-done | bytes 262176 | tf_op jit(solution)/shard_map/ppermute | solution.py:13
  32.0 2.2 all_gather.35
  34.1 2.5 collective-permute-done.2
  37.8 3.2 collective-permute-done.3
  42.6 2.2 all_gather.36
  46.8 9.2 %scatter_fusion = f32[7168,128]{1,0:T(8,128)} fusion(f32[7168,128]{1,0:T(8,128)} %scatter_custom_fusion, s32[1024]{0:T(1024)S(1)} %bitcast.46, f32[1024,128]{1,0:T(8,128)S(1)} %copy.48), kind=kCustom, calls=%fused_computation.4 | custom fusion | flops 131072 | bytes 1576960 | tf_op jit(solution)/shard_map/scatter-add | solution.py:114
  59.5 11.6 %collective-permute-done.5 = f32[1024,128]{0,1:T(8,128)S(1)} collective-permute-done((f32[1024,128]{0,1:T(8,128)S(1)}, f32[1024,128]{0,1:T(8,128)S(1)}, u32[]{:S(2)}, u32[]{:S(2)}) %collective-permute-start.5) | collective-permute-done | bytes 524320 | tf_op jit(solution)/shard_map/ppermute | solution.py:13
  71.9 6.1 %collective-permute-done.6 = f32[512,128]{0,1:T(8,128)S(1)} collective-permute-done((f32[512,128]{0,1:T(8,128)S(1)}, f32[512,128]{0,1:T(8,128)S(1)}, u32[]{:S(2)}, u32[]{:S(2)}) %collective-permute-start.6) | collective-permute-done | bytes 262176 | tf_op jit(solution)/shard_map/ppermute | solution.py:13
  79.0 4.2 collective-permute-done.7
  85.2 55.7 %all-gather.8.cloned.1.call-done = bf16[4096,128]{0,1:T(8,128)(2,1)} async-done(((bf16[256,128]{0,1:T(8,128)(2,1)}), bf16[4096,128]{0,1:T(8,128)(2,1)}) %all-gather.8.cloned.1.call-update) | async-done | bytes 1048592 | tf_op jit(solution)/shard_map/all_gather | solution.py:32
  141.0 1.9 convolution_convert_fusion.1
  142.8 7.6 %all-gather.12.cloned.1.call-done = bf16[256,2048]{1,0:T(8,128)(2,1)} async-done(((bf16[128,2048]{1,0:T(8,128)(2,1)}), bf16[256,2048]{1,0:T(8,128)(2,1)}) %all-gather.12.cloned.1.call-update) | async-done | bytes 1048592 | tf_op jit(solution)/shard_map/all_gather | solution.py:89
  152.3 14.1 %scatter_fusion.1 = f32[7168,128]{1,0:T(8,128)} fusion(f32[7168,128]{1,0:T(8,128)} %scatter_fusion, s32[2048]{0:T(1024)S(1)} %bitcast.44, f32[2048,128]{1,0:T(8,128)S(1)} %copy.52), kind=kCustom, calls=%fused_computation.5 | custom fusion | flops 262144 | bytes 3153920 | tf_op jit(solution)/shard_map/scatter-add | solution.py:114
  168.9 2.7 collective-permute-start.8
  171.7 46.1 %collective-permute-done.8 = f32[2048,128]{0,1:T(8,128)S(1)} collective-permute-done((f32[2048,128]{0,1:T(8,128)S(1)}, f32[2048,128]{0,1:T(8,128)S(1)}, u32[]{:S(2)}, u32[]{:S(2)}) %collective-permute-start.8) | collective-permute-done | bytes 1048608 | tf_op jit(solution)/shard_map/ppermute | solution.py:13
  219.1 12.4 %collective-permute-done.9 = f32[1024,128]{0,1:T(8,128)S(1)} collective-permute-done((f32[1024,128]{0,1:T(8,128)S(1)}, f32[1024,128]{0,1:T(8,128)S(1)}, u32[]{:S(2)}, u32[]{:S(2)}) %collective-permute-start.9) | collective-permute-done | bytes 524320 | tf_op jit(solution)/shard_map/ppermute | solution.py:13
  231.6 1.7 collective-permute-start.10
  233.3 5.1 collective-permute-done.10
  238.6 1.7 collective-permute-start.11
  240.4 3.2 collective-permute-done.11
  244.4 57.4 %all-gather.14.cloned.1.call-done = bf16[4096,128]{0,1:T(8,128)(2,1)} async-done(((bf16[256,128]{0,1:T(8,128)(2,1)}), bf16[4096,128]{0,1:T(8,128)(2,1)}) %all-gather.14.cloned.1.call-update) | async-done | bytes 1048592 | tf_op jit(solution)/shard_map/all_gather | solution.py:32
  301.8 4.2 convolution_bitcast_fusion
  307.2 45.2 %collective-permute-done.12 = f32[2048,128]{0,1:T(8,128)S(1)} collective-permute-done((f32[2048,128]{0,1:T(8,128)S(1)}, f32[2048,128]{0,1:T(8,128)S(1)}, u32[]{:S(2)}, u32[]{:S(2)}) %collective-permute-start.12) | collective-permute-done | bytes 1048608 | tf_op jit(solution)/shard_map/ppermute | solution.py:13
  352.7 13.8 %collective-permute-done.13 = f32[1024,128]{0,1:T(8,128)S(1)} collective-permute-done((f32[1024,128]{0,1:T(8,128)S(1)}, f32[1024,128]{0,1:T(8,128)S(1)}, u32[]{:S(2)}, u32[]{:S(2)}) %collective-permute-start.13) | collective-permute-done | bytes 524320 | tf_op jit(solution)/shard_map/ppermute | solution.py:13
  368.1 6.0 %collective-permute-done.14 = f32[512,128]{0,1:T(8,128)S(1)} collective-permute-done((f32[512,128]{0,1:T(8,128)S(1)}, f32[512,128]{0,1:T(8,128)S(1)}, u32[]{:S(2)}, u32[]{:S(2)}) %collective-permute-start.14) | collective-permute-done | bytes 262176 | tf_op jit(solution)/shard_map/ppermute | solution.py:13
  375.2 4.1 collective-permute-done.15
  380.1 52.8 %all-gather.18.cloned.1.call-done = bf16[4096,128]{0,1:T(8,128)(2,1)} async-done(((bf16[256,128]{0,1:T(8,128)(2,1)}), bf16[4096,128]{0,1:T(8,128)(2,1)}) %all-gather.18.cloned.1.call-update) | async-done | bytes 1048592 | tf_op jit(solution)/shard_map/all_gather | solution.py:32
  434.2 2.3 copy.55
  436.6 9.4 %gather_fusion = bf16[2048,128]{1,0:T(8,128)(2,1)} fusion(bf16[7168,128]{1,0:T(8,128)(2,1)} %copy.55, s32[2048]{0:T(1024)S(1)} %broadcast_clamp_fusion), kind=kCustom, calls=%fused_computation | custom fusion | bytes 1056768 | tf_op jit(solution)/shard_map/jit(_take)/gather | solution.py:123
  446.0 3.1 convolution_bitcast_fusion.1
  449.2 2.5 collective-permute-start.16
  451.7 9.4 %collective-permute-done.16 = f32[1024,128]{0,1:T(8,128)S(1)} collective-permute-done((f32[1024,128]{0,1:T(8,128)S(1)}, f32[1024,128]{0,1:T(8,128)S(1)}, u32[]{:S(2)}, u32[]{:S(2)}) %collective-permute-start.16) | collective-permute-done | bytes 524320 | tf_op jit(solution)/shard_map/ppermute | solution.py:13
  462.6 5.1 collective-permute-done.17
  469.1 3.7 collective-permute-done.18
  474.0 55.5 %all-gather.20.cloned.1.call-done = bf16[4096,128]{0,1:T(8,128)(2,1)} async-done(((bf16[256,128]{0,1:T(8,128)(2,1)}), bf16[4096,128]{0,1:T(8,128)(2,1)}) %all-gather.20.cloned.1.call-update) | async-done | bytes 1048592 | tf_op jit(solution)/shard_map/all_gather | solution.py:32
  530.6 2.3 copy.56
  533.0 4.7 gather_fusion.1
  537.7 1.9 convolution_bitcast_fusion.3
  540.3 5.7 collective-permute-done.19
  547.4 4.5 collective-permute-done.20
  553.1 3.1 collective-permute-done.21
  557.6 3.7 collective-permute-done.22
  561.4 2.3 copy.57
  563.7 2.8 gather_fusion.2
  (156 shorter events, 47.6 us)
Async XLA Ops:
  7.2 78.1 %all-gather.10.cloned.1.call-start = ((), (), s32[]{:S(2)}) async-start(), calls=%async_computation.1 | async-start | bytes 1572864 | tf_op jit(solution)/shard_map/all_gather | solution.py:86
  8.2 8.7 %collective-permute-start = (bf16[256,128]{0,1:T(8,128)(2,1)S(1)}, bf16[256,128]{0,1:T(8,128)(2,1)S(1)}, u32[]{:S(2)}, u32[]{:S(2)}) collective-permute-start(bf16[256,128]{0,1:T(8,128)(2,1)S(1)} %copy.41), channel_id=1, source_target_pairs={{0,2},{2,0},{4,6},{6,4},{8,10},{10,8},{12,14},{14,12},{16,18},{18,... | collective-permute-start | bytes 196616 | tf_op jit(solution)/shard_map/ppermute | solution.py:13
  13.4 8.3 %copy-start.3 = (bf16[256,512]{1,0:T(8,128)(2,1)}, bf16[256,512]{1,0:T(8,128)(2,1)S(1)}, u32[]{:S(2)}) copy-start(bf16[256,512]{1,0:T(8,128)(2,1)S(1)} %all_gather.33) | copy-start | bytes 786436
  21.6 10.3 %copy-start.7 = (bf16[128,1024]{1,0:T(8,128)(2,1)S(1)}, bf16[128,1024]{1,0:T(8,128)(2,1)}, u32[]{:S(2)}) copy-start(bf16[128,1024]{1,0:T(8,128)(2,1)} %param.26) | copy-start | bytes 786436
  23.0 19.6 %copy-start.8 = (bf16[128,1024]{1,0:T(8,128)(2,1)S(1)}, bf16[128,1024]{1,0:T(8,128)(2,1)}, u32[]{:S(2)}) copy-start(bf16[128,1024]{1,0:T(8,128)(2,1)} %param.29) | copy-start | bytes 786436
  23.1 8.4 %collective-permute-start.1 = (f32[512,128]{0,1:T(8,128)S(1)}, f32[512,128]{0,1:T(8,128)S(1)}, u32[]{:S(2)}, u32[]{:S(2)}) collective-permute-start(f32[512,128]{0,1:T(8,128)S(1)} %broadcast_select_fusion.2), channel_id=1, source_target_pairs={{0,4},{2,6},{4,0},{6,2},{8,12},{10,14},{12,8},{14,10},{16,20},{18,... | collective-permute-start | bytes 786440 | tf_op jit(solution)/shard_map/ppermute | solution.py:13
  31.6 5.0 collective-permute-start.2
  34.1 11.9 %copy-start.2 = (bf16[256,1024]{1,0:T(8,128)(2,1)}, bf16[256,1024]{1,0:T(8,128)(2,1)S(1)}, u32[]{:S(2)}) copy-start(bf16[256,1024]{1,0:T(8,128)(2,1)S(1)} %all_gather.35) | copy-start | bytes 1572868
  36.7 4.3 collective-permute-start.3
  41.0 5.0 collective-permute-start.4
  46.4 9.7 %copy-start.9 = (bf16[128,256]{1,0:T(8,128)(2,1)}, bf16[128,256]{1,0:T(8,128)(2,1)S(1)}, u32[]{:S(2)}) copy-start(bf16[128,256]{1,0:T(8,128)(2,1)S(1)} %convolution_convert_fusion.2) | copy-start | bytes 196612
  57.8 21.0 %copy-start.12 = (bf16[256,128]{1,0:T(8,128)(2,1)S(1)}, bf16[256,128]{1,0:T(8,128)(2,1)}, u32[]{:S(2)}) copy-start(bf16[256,128]{1,0:T(8,128)(2,1)} %param.21) | copy-start | bytes 196612
  57.8 13.3 %collective-permute-start.5 = (f32[1024,128]{0,1:T(8,128)S(1)}, f32[1024,128]{0,1:T(8,128)S(1)}, u32[]{:S(2)}, u32[]{:S(2)}) collective-permute-start(f32[1024,128]{0,1:T(8,128)S(1)} %broadcast_select_fusion.1), channel_id=1, source_target_pairs={{0,8},{2,10},{4,12},{6,14},{8,0},{10,2},{12,4},{14,6},{16,24},{18,... | collective-permute-start | bytes 1572872 | tf_op jit(solution)/shard_map/ppermute | solution.py:13
  71.2 13.4 %copy-start.19 = (s32[2,2048]{1,0:T(2,128)S(1)}, s32[2,2048]{1,0:T(2,128)}, u32[]{:S(2)}) copy-start(s32[2,2048]{1,0:T(2,128)} %param.31) | copy-start | bytes 49156
  71.3 6.7 %collective-permute-start.6 = (f32[512,128]{0,1:T(8,128)S(1)}, f32[512,128]{0,1:T(8,128)S(1)}, u32[]{:S(2)}, u32[]{:S(2)}) collective-permute-start(f32[512,128]{0,1:T(8,128)S(1)} %slice_select_fusion.8), channel_id=1, source_target_pairs={{0,4},{2,6},{4,0},{6,2},{8,12},{10,14},{12,8},{14,10},{16,20},{18,... | collective-permute-start | bytes 786440 | tf_op jit(solution)/shard_map/ppermute | solution.py:13
  71.9 69.1 %all-gather.8.cloned.1.call-start = ((), (), s32[]{:S(2)}) async-start(), calls=%async_computation | async-start | bytes 1114112 | tf_op jit(solution)/shard_map/all_gather | solution.py:32
  78.1 5.0 collective-permute-start.7
  83.8 66.6 %all-gather.12.cloned.1.call-start = ((), (), s32[]{:S(2)}) async-start(), calls=%async_computation.2 | async-start | bytes 1572864 | tf_op jit(solution)/shard_map/all_gather | solution.py:89
  84.5 159.8 %all-gather.16.cloned.1.call-start = ((), (), s32[]{:S(2)}) async-start(), calls=%async_computation.4 | async-start | bytes 3145728 | tf_op jit(solution)/shard_map/all_gather | solution.py:85
  168.9 48.8 %collective-permute-start.8 = (f32[2048,128]{0,1:T(8,128)S(1)}, f32[2048,128]{0,1:T(8,128)S(1)}, u32[]{:S(2)}, u32[]{:S(2)}) collective-permute-start(f32[2048,128]{0,1:T(8,128)S(1)} %broadcast_select_fusion), channel_id=1, source_target_pairs={{0,16},{2,18},{4,20},{6,22},{8,24},{10,26},{12,28},{14,30},{16,0},... | collective-permute-start | bytes 3145736 | tf_op jit(solution)/shard_map/ppermute | solution.py:13
  218.1 13.4 %collective-permute-start.9 = (f32[1024,128]{0,1:T(8,128)S(1)}, f32[1024,128]{0,1:T(8,128)S(1)}, u32[]{:S(2)}, u32[]{:S(2)}) collective-permute-start(f32[1024,128]{0,1:T(8,128)S(1)} %slice_select_fusion.3), channel_id=1, source_target_pairs={{0,8},{2,10},{4,12},{6,14},{8,0},{10,2},{12,4},{14,6},{16,24},{18,... | collective-permute-start | bytes 1572872 | tf_op jit(solution)/shard_map/ppermute | solution.py:13
  218.9 21.4 %copy-start.13 = (bf16[256,128]{1,0:T(8,128)(2,1)S(1)}, bf16[256,128]{1,0:T(8,128)(2,1)}, u32[]{:S(2)}) copy-start(bf16[256,128]{1,0:T(8,128)(2,1)} %param.20) | copy-start | bytes 196612
  218.9 82.9 %all-gather.14.cloned.1.call-start = ((), (), s32[]{:S(2)}) async-start(), calls=%async_computation.3 | async-start | bytes 1114112 | tf_op jit(solution)/shard_map/all_gather | solution.py:32
  231.6 6.9 %collective-permute-start.10 = (f32[512,128]{0,1:T(8,128)S(1)}, f32[512,128]{0,1:T(8,128)S(1)}, u32[]{:S(2)}, u32[]{:S(2)}) collective-permute-start(f32[512,128]{0,1:T(8,128)S(1)} %slice_select_fusion.7), channel_id=1, source_target_pairs={{0,4},{2,6},{4,0},{6,2},{8,12},{10,14},{12,8},{14,10},{16,20},{18,... | collective-permute-start | bytes 786440 | tf_op jit(solution)/shard_map/ppermute | solution.py:13
  238.6 5.0 collective-permute-start.11
  244.3 188.5 %all-gather.18.cloned.1.call-start = ((), (), s32[]{:S(2)}) async-start(), calls=%async_computation.5 | async-start | bytes 1114112 | tf_op jit(solution)/shard_map/all_gather | solution.py:32
  306.1 46.3 %collective-permute-start.12 = (f32[2048,128]{0,1:T(8,128)S(1)}, f32[2048,128]{0,1:T(8,128)S(1)}, u32[]{:S(2)}, u32[]{:S(2)}) collective-permute-start(f32[2048,128]{0,1:T(8,128)S(1)} %slice_select_fusion), channel_id=1, source_target_pairs={{0,16},{2,18},{4,20},{6,22},{8,24},{10,26},{12,28},{14,30},{16,0},... | collective-permute-start | bytes 3145736 | tf_op jit(solution)/shard_map/ppermute | solution.py:13
  352.6 27.4 %copy-start.14 = (s32[1,2048]{1,0:T(1,128)S(1)}, s32[1,2048]{1,0:T(1,128)}, u32[]{:S(2)}) copy-start(s32[1,2048]{1,0:T(1,128)} %get-tuple-element.49) | copy-start | bytes 24580
  352.7 13.9 %collective-permute-start.13 = (f32[1024,128]{0,1:T(8,128)S(1)}, f32[1024,128]{0,1:T(8,128)S(1)}, u32[]{:S(2)}, u32[]{:S(2)}) collective-permute-start(f32[1024,128]{0,1:T(8,128)S(1)} %slice_select_fusion.2), channel_id=1, source_target_pairs={{0,8},{2,10},{4,12},{6,14},{8,0},{10,2},{12,4},{14,6},{16,24},{18,... | collective-permute-start | bytes 1572872 | tf_op jit(solution)/shard_map/ppermute | solution.py:13
  366.7 7.4 %collective-permute-start.14 = (f32[512,128]{0,1:T(8,128)S(1)}, f32[512,128]{0,1:T(8,128)S(1)}, u32[]{:S(2)}, u32[]{:S(2)}) collective-permute-start(f32[512,128]{0,1:T(8,128)S(1)} %slice_select_fusion.6), channel_id=1, source_target_pairs={{0,4},{2,6},{4,0},{6,2},{8,12},{10,14},{12,8},{14,10},{16,20},{18,... | collective-permute-start | bytes 786440 | tf_op jit(solution)/shard_map/ppermute | solution.py:13
  374.3 5.0 collective-permute-start.15
  380.0 149.6 %all-gather.20.cloned.1.call-start = ((), (), s32[]{:S(2)}) async-start(), calls=%async_computation.6 | async-start | bytes 1114112 | tf_op jit(solution)/shard_map/all_gather | solution.py:32
  449.2 12.0 %collective-permute-start.16 = (f32[1024,128]{0,1:T(8,128)S(1)}, f32[1024,128]{0,1:T(8,128)S(1)}, u32[]{:S(2)}, u32[]{:S(2)}) collective-permute-start(f32[1024,128]{0,1:T(8,128)S(1)} %slice_select_fusion.1), channel_id=1, source_target_pairs={{0,8},{2,10},{4,12},{6,14},{8,0},{10,2},{12,4},{14,6},{16,24},{18,... | collective-permute-start | bytes 1572872 | tf_op jit(solution)/shard_map/ppermute | solution.py:13
  461.3 6.4 %collective-permute-start.17 = (f32[512,128]{0,1:T(8,128)S(1)}, f32[512,128]{0,1:T(8,128)S(1)}, u32[]{:S(2)}, u32[]{:S(2)}) collective-permute-start(f32[512,128]{0,1:T(8,128)S(1)} %slice_select_fusion.5), channel_id=1, source_target_pairs={{0,4},{2,6},{4,0},{6,2},{8,12},{10,14},{12,8},{14,10},{16,20},{18,... | collective-permute-start | bytes 786440 | tf_op jit(solution)/shard_map/ppermute | solution.py:13
  467.8 5.0 collective-permute-start.18
  533.0 4.7 copy-start.1
  533.0 4.7 copy-start.10
  533.0 4.7 copy-start.18
  537.7 19.8 %copy-start.17 = (s32[1,512]{1,0:T(1,128)S(1)}, s32[1,512]{1,0:T(1,128)}, u32[]{:S(2)}) copy-start(s32[1,512]{1,0:T(1,128)} %get-tuple-element.53) | copy-start | bytes 6148
  537.7 19.8 %copy-start.16 = (s32[512,1]{0,1:T(1,128)S(1)}, s32[512,1]{0,1:T(1,128)}, u32[]{:S(2)}) copy-start(s32[512,1]{0,1:T(1,128)} %copy-done.15) | copy-start | bytes 6148
  539.6 6.4 %collective-permute-start.19 = (f32[512,128]{0,1:T(8,128)S(1)}, f32[512,128]{0,1:T(8,128)S(1)}, u32[]{:S(2)}, u32[]{:S(2)}) collective-permute-start(f32[512,128]{0,1:T(8,128)S(1)} %slice_select_fusion.4), channel_id=1, source_target_pairs={{0,4},{2,6},{4,0},{6,2},{8,12},{10,14},{12,8},{14,10},{16,20},{18,... | collective-permute-start | bytes 786440 | tf_op jit(solution)/shard_map/ppermute | solution.py:13
  546.1 5.7 collective-permute-start.20
  551.9 4.3 collective-permute-start.21
  556.3 5.0 collective-permute-start.22
  561.4 5.2 copy-start.4
  563.7 4.7 copy-start.5
  563.7 5.4 copy-start.6
  567.1 5.0 collective-permute-start.23
  (3 other events, 7.4 us)
Sparse Core Ops, SparseCore 0:
  72.0 9.3 all-gather.9
  84.7 56.2 all-gather.7
  142.5 7.8 all-gather.11
  219.0 11.5 all-gather.15
  244.4 57.3 all-gather.13
  380.1 52.6 all-gather.17
  473.6 55.8 all-gather.19
where the time goes:
time: 581 us; the launch traced here: 580 us
  waiting for transfers between devices  438 us (75%)
  local copies, waits for them, and re-layouts  36.7 us (6%)
  other arithmetic  35.6 us (6%)
  starting transfers between devices  31.9 us (5%)
  between operations  14.8 us (3%)
  matrix products  14 us (2%)
  blocking collectives  8.72 us (2%)
    all_gather x4, waiting for transfers between devices, collect_rows(): gathered = lax.all_gather(own_block, 'leaf', axis=0, tiled=True)  221 us
    ppermute x24, waiting for transfers between devices, swapped(): return lax.ppermute(value, axis, pairs)  208 us
    ppermute x24, starting transfers between devices, swapped(): return lax.ppermute(value, axis, pairs)  31.4 us
    scatter-add x3, other arithmetic, body(): accumulated = accumulated.at[row_list].add(update)  27.6 us
    gather x3, local copies, waits for them, and re-layouts, body(): picked = jnp.take(anc_values, row_list, axis=0)  16.9 us
  transfers between devices with their start and end apart: 31, of which 28 were waited for; matrix products, arithmetic and copies ran while one was open for 2% of the time, Pallas kernels for 0%

commit v1 on v0

v1 whole, which is shorter than its diff:
```python
import functools

import jax
import jax.numpy as jnp
from jax import lax
from jax.experimental import pallas as pl
from jax.experimental.pallas import tpu as pltpu
from jax.sharding import PartitionSpec as P

LEVELS = 4
MESH = pl.DeviceIdType.MESH


def split_group(groups):
    high = 1
    low = groups
    while low > 8 or (high > 1 and low > 4 and high < 4):
        low //= 2
        high *= 2
    if high > 1 and high < low:
        low, high = low // 2, high * 2
    return low, high


def exchange_kernel(groups, reduce, gather, has_extra, *refs):
    refs = list(refs)
    part_ref = refs.pop(0) if reduce else None
    extra_ref = refs.pop(0) if has_extra else None
    own_ref = refs.pop(0)
    full_ref = refs.pop(0) if gather else None
    if reduce:
        low_buf, high_buf, high_out, rs_send, rs_recv, rz_send, rz_recv = refs[:7]
        refs = refs[7:]
    if gather:
        ag_send, ag_recv, az_send, az_recv = refs[:4]
    low, high = split_group(groups)
    rows = own_ref.shape[0]
    me = lax.axis_index("leaf")
    panel = lax.axis_index("panel")
    base = me // groups * groups
    mine = me - base
    my_low = lax.rem(mine, low)
    my_high = mine // low

    def leaf_of(high_part, low_part):
        return base + high_part * low + low_part

    def low_peer(step):
        return leaf_of(my_high, my_low ^ step)

    def high_peer(step):
        return leaf_of(my_high ^ step, my_low)

    def block(ref, high_part, low_part):
        start = (high_part * low + low_part) * rows
        return ref.at[pl.ds(pl.multiple_of(start, rows), rows)]

    def remote(src, dst, send, recv, leaf):
        return pltpu.make_async_remote_copy(
            src_ref=src, dst_ref=dst, send_sem=send, recv_sem=recv,
            device_id=(leaf, panel), device_id_type=MESH,
        )

    barrier = pltpu.get_barrier_semaphore()
    for step in range(1, low):
        pl.semaphore_signal(barrier, inc=1, device_id=(low_peer(step), panel), device_id_type=MESH)
    for step in range(1, high):
        pl.semaphore_signal(barrier, inc=1, device_id=(high_peer(step), panel), device_id_type=MESH)
    pl.semaphore_wait(barrier, low + high - 2)

    pending = []
    order = list(range(high - 1, 0, -1)) + [0]
    if reduce:
        low_copies = {}
        for plane in order:
            for step in range(low - 1, 0, -1):
                copy = remote(
                    block(part_ref, my_high ^ plane, my_low ^ step),
                    low_buf.at[plane, step - 1],
                    rs_send.at[plane, step - 1], rs_recv.at[plane, step - 1],
                    low_peer(step),
                )
                copy.start()
                low_copies[plane, step] = copy
        high_copies = {}
        for plane in order:
            total = block(part_ref, my_high ^ plane, my_low)[...].astype(jnp.float32)
            if plane == 0 and has_extra:
                total = total + extra_ref[...].astype(jnp.float32)
            for step in range(1, low):
                low_copies[plane, step].wait_recv()
                total = total + low_buf[plane, step - 1].astype(jnp.float32)
            if plane:
                high_out[plane - 1] = total.astype(jnp.bfloat16)
                copy = remote(
                    high_out.at[plane - 1], high_buf.at[plane - 1],
                    rz_send.at[plane - 1], rz_recv.at[plane - 1],
                    high_peer(plane),
                )
                copy.start()
                high_copies[plane] = copy
        for plane in range(1, high):
            high_copies[plane].wait_recv()
            total = total + high_buf[plane - 1].astype(jnp.float32)
        own_ref[...] = total.astype(jnp.bfloat16)
        pending += list(low_copies.values()) + list(high_copies.values())
    else:
        own_ref[...] = extra_ref[...]
    if gather:
        block(full_ref, my_high, my_low)[...] = own_ref[...]
        arriving = {}
        for plane in order[:-1]:
            copy = remote(
                own_ref, block(full_ref, my_high, my_low),
                az_send.at[plane - 1], az_recv.at[plane - 1], high_peer(plane),
            )
            copy.start()
            pending.append(copy)
            arriving[plane] = copy
        forwards = []
        for plane in range(high):
            if plane:
                arriving[plane].wait_recv()
            for step in range(low - 1, 0, -1):
                here = block(full_ref, my_high ^ plane, my_low)
                copy = remote(
                    here if plane else own_ref, here,
                    ag_send.at[plane, step - 1], ag_recv.at[plane, step - 1], low_peer(step),
                )
                copy.start()
                pending.append(copy)
                forwards.append(copy)
        for copy in forwards:
            copy.wait_recv()
    for copy in pending:
        copy.wait_send()


def exchange(groups, part, extra, gather, ident):
    reduce = part is not None
    low, high = split_group(groups)
    if reduce:
        rows, columns = part.shape[0] // groups, part.shape[1]
    else:
        rows, columns = extra.shape
    own = jax.ShapeDtypeStruct((rows, columns), jnp.bfloat16)
    full = jax.ShapeDtypeStruct((rows * groups, columns), jnp.bfloat16)
    highs = max(high - 1, 1)
    dma = pltpu.SemaphoreType.DMA
    scratch = []
    if reduce:
        scratch += [
            pltpu.VMEM((high, low - 1, rows, columns), jnp.bfloat16),
            pltpu.VMEM((highs, rows, columns), jnp.bfloat16),
            pltpu.VMEM((highs, rows, columns), jnp.bfloat16),
            dma((high, low - 1)), dma((high, low - 1)), dma((highs,)), dma((highs,)),
        ]
    if gather:
        scratch += [dma((high, low - 1)), dma((high, low - 1)), dma((highs,)), dma((highs,))]
    operands = [value for value in (part, extra) if value is not None]
    outs = (own, full) if gather else (own,)
    vmem = pl.BlockSpec(memory_space=pltpu.VMEM)
    return pl.pallas_call(
        functools.partial(exchange_kernel, groups, reduce, gather, extra is not None),
        out_shape=outs,
        in_specs=[vmem] * len(operands),
        out_specs=tuple([vmem] * len(outs)),
        scratch_shapes=scratch,
        compiler_params=pltpu.CompilerParams(
            collective_id=ident, has_side_effects=True, vmem_limit_bytes=32 * 2**20
        ),
    )(*operands)


def contract_rows(left, right):
    return lax.dot_general(
        left, right, (((0,), (0,)), ((), ())), preferred_element_type=jnp.float32
    )


def body(
    rhs_0, rhs_1, rhs_2, rhs_3,
    inv_0, inv_1, inv_2, inv_3,
    coupling_1, coupling_2, coupling_3,
    update_rows_1, update_rows_2, update_rows_3,
):
    rhs_all = [rhs_0, rhs_1, rhs_2, rhs_3]
    lists_all = [None, update_rows_1, update_rows_2, update_rows_3]
    columns = rhs_0.shape[1]
    leaf_count = lax.axis_size("leaf")
    front_sizes = [inv_0.shape[1], inv_1.shape[1], inv_2.shape[1], inv_3.shape[1]]
    offsets = [0]
    for depth_now in range(1, LEVELS):
        offsets.append(offsets[-1] + front_sizes[depth_now - 1])

    def whole_rows(value):
        return lax.all_gather(value, "panel", axis=0, tiled=True)

    inv_3, coupling_3 = whole_rows(inv_3), whole_rows(coupling_3)
    inv_2, coupling_2 = whole_rows(inv_2), whole_rows(coupling_2)
    inv_1, coupling_1 = whole_rows(inv_1), whole_rows(coupling_1)
    inv_all = [whole_rows(inv_0), inv_1, inv_2, inv_3]
    coup_all = [None, coupling_1, coupling_2, coupling_3]
    accumulated = jnp.zeros((offsets[LEVELS - 1], columns), jnp.float32)
    forwards = [None] * LEVELS
    row_lists = [None] * LEVELS
    for depth_now in reversed(range(LEVELS)):
        groups = leaf_count >> depth_now
        front_rows = front_sizes[depth_now]
        front = lax.axis_index("leaf") // groups
        part = None
        if depth_now < LEVELS - 1:
            start = offsets[depth_now]
            part = accumulated[start : start + front_rows].astype(jnp.bfloat16)
        _, combined = exchange(groups, part, rhs_all[depth_now], True, depth_now)
        values = jnp.dot(
            inv_all[depth_now], combined, preferred_element_type=jnp.float32
        ).astype(jnp.bfloat16)
        forwards[depth_now] = values
        if depth_now > 0:
            update = contract_rows(coup_all[depth_now], values)
            row_lists[depth_now] = lax.dynamic_index_in_dim(
                lists_all[depth_now], front, 0, keepdims=False
            )
            accumulated = accumulated.at[row_lists[depth_now]].add(update)
    anc_values = []
    outputs = []
    for depth_now in range(LEVELS):
        groups = leaf_count >> depth_now
        adjusted = forwards[depth_now]
        if depth_now > 0:
            picked = jnp.take(jnp.concatenate(anc_values, axis=0), row_lists[depth_now], axis=0)
            pulled = jnp.dot(coup_all[depth_now], picked, preferred_element_type=jnp.float32)
            adjusted = (adjusted.astype(jnp.float32) - pulled).astype(jnp.bfloat16)
        partial_value = contract_rows(inv_all[depth_now], adjusted).astype(jnp.bfloat16)
        last = depth_now == LEVELS - 1
        found = exchange(groups, partial_value, None, not last, LEVELS + depth_now)
        outputs.append(found[0])
        if not last:
            anc_values.append(found[1])
    return tuple(outputs)


def solution(mesh):
    in_specs = (P("leaf", "panel"),) * 4 + (P(("leaf", "panel"), None),) * 7 + (P(),) * 3
    out_specs = (P("leaf", "panel"),) * 4
    return jax.shard_map(body, mesh=mesh, in_specs=in_specs, out_specs=out_specs, check_vma=False)
```

time: 581 us -> 220 us (0.38)
  waiting for transfers between devices: 438 us -> 2.12 us
  Pallas kernels: 0 us -> 127 us
  starting transfers between devices: 31.9 us -> 0.11 us
  local copies, waits for them, and re-layouts: 36.7 us -> 21.5 us
    all_gather x7 -> x3, waiting for transfers between devices: 229 us -> 0.06 us  [whole_rows(): return lax.all_gather(value, 'panel', axis=0, tiled=True)]
    ppermute x24 -> x0, waiting for transfers between devices: 208 us -> none  [swapped(): return lax.ppermute(value, axis, pairs)]
    pallas_call x0 -> x8, Pallas kernels: none -> 127 us  [exchange(): pl.pallas_call(functools.partial(exchange_kernel, groups, reduce, gather,...]
    ppermute x24 -> x0, starting transfers between devices: 31.4 us -> none  [swapped(): return lax.ppermute(value, axis, pairs)]
    scatter x5 -> x0, local copies, waits for them, and re-layouts: 9.44 us -> none  [body(): anc_values.at[offsets[depth_now]:offsets[depth_now] + front_rows]]
  transfers between devices with their start and end apart: 31 -> 3, of which waited for: 28 -> 0; matrix products, arithmetic and copies ran while one was open for 2% -> 18% of each run, Pallas kernels for 0% -> 31%
where the time goes in v1:
time: 220 us; the launch traced here: 219 us
  Pallas kernels  127 us (58%)
  other arithmetic  31.2 us (14%)
  local copies, waits for them, and re-layouts  21.5 us (10%)
  matrix products  14.9 us (7%)
  between operations  14.2 us (6%)
  blocking collectives  8.95 us (4%)
    pallas_call x8, Pallas kernels, exchange(): pl.pallas_call(functools.partial(exchange_kernel, groups, reduce, gather,...  127 us
    scatter-add x3, other arithmetic, body(): accumulated = accumulated.at[row_lists[depth_now]].add(update)  27.6 us
    gather x3, local copies, waits for them, and re-layouts, body(): jnp.take(jnp.concatenate(anc_values, axis=0), row_lists[depth_now], axis=0)  13.2 us
    dot_general x7, matrix products, contract_rows(): lax.dot_general(left, right, (((0,), (0,)), ((), ())), preferred_element_...  12.7 us
    all_gather x4, blocking collectives, whole_rows(): return lax.all_gather(value, 'panel', axis=0, tiled=True)  8.95 us
  transfers between devices with their start and end apart: 3, of which 0 were waited for; matrix products, arithmetic and copies ran while one was open for 18% of the time, Pallas kernels for 31%

profile of v1, /device:TPU:0, one launch (start us, length us, event | category | flops | bytes accessed | tf_op | source)
XLA Modules:
  0.0 219.4 jit_solution(7147555842811989941)
XLA Ops:
  7.2 0.7 all-gather.4.cloned.1.call-update
  7.9 0.7 all-gather.6.cloned.1.call-update
  8.6 0.0 all-gather.8.cloned.1.call-start
  8.7 0.7 all-gather.8.cloned.1.call-update
  9.4 2.3 %all_gather.21 = bf16[256,512]{1,0:T(8,128)(2,1)S(1)} all-gather(bf16[128,512]{1,0:T(8,128)(2,1)} %param.21), channel_id=1, replica_groups=mesh['leaf'=16,'panel'=2] {'panel'}, dimensions={0}, use_global_device_ids=true | all-gather | bytes 393216 | tf_op jit(solution)/shard_map/all_gather | solution.py:197
  11.7 0.8 copy-done.3
  12.6 5.9 %shard_map.165 = (bf16[256,128]{1,0:T(8,128)(2,1)}, bf16[512,128]{1,0:T(8,128)(2,1)S(1)}) custom-call(bf16[256,128]{1,0:T(8,128)(2,1)S(1)} %copy-done.3), custom_call_target="tpu_custom_call" | custom-call | tf_op jit(solution)/shard_map/pallas_call | solution.py:163
  18.5 2.3 %all_gather.22 = bf16[256,512]{1,0:T(8,128)(2,1)S(1)} all-gather(bf16[128,512]{1,0:T(8,128)(2,1)} %param.24), channel_id=1, replica_groups=mesh['leaf'=16,'panel'=2] {'panel'}, dimensions={0}, use_global_device_ids=true | all-gather | bytes 393216 | tf_op jit(solution)/shard_map/all_gather | solution.py:197
  20.8 0.2 convolution_convert_fusion.7
  21.0 0.5 copy-done.9
  21.5 0.2 convolution_bitcast_fusion.2
  21.7 0.1 copy.24
  21.9 0.7 compare_select_fusion.5
  22.6 4.2 %scatter_custom_fusion = f32[7168,128]{1,0:T(8,128)} fusion(s32[512]{0:T(512)S(1)} %bitcast.66, f32[512,128]{1,0:T(8,128)S(1)} %copy.24, f32[]{:T(128)} %constant.88.clone.1), kind=kCustom, calls=%fused_computation.13 | custom fusion | flops 65536 | bytes 3670020 | tf_op jit(solution)/shard_map/scatter-add | solution.py:225
  26.8 1.1 slice.29.refs_0_
  27.9 2.2 all_gather.23
  30.1 2.2 all_gather.24
  32.3 12.4 %shard_map.166 = (bf16[256,128]{1,0:T(8,128)(2,1)}, bf16[1024,128]{1,0:T(8,128)(2,1)S(1)}) custom-call(bf16[1024,128]{1,0:T(8,128)(2,1)S(1)} %slice.29.refs_0_, bf16[256,128]{1,0:T(8,128)(2,1)S(1)} %copy-done), custom_call_target="tpu_custom_call" | custom-call | tf_op jit(solution)/shard_map/pallas_call | solution.py:163
  44.6 0.3 convolution_convert_fusion.6
  45.0 0.2 convolution_bitcast_fusion.1
  45.2 0.2 copy.25
  45.4 0.7 compare_select_fusion.2
  46.2 9.3 %scatter_fusion = f32[7168,128]{1,0:T(8,128)} fusion(f32[7168,128]{1,0:T(8,128)} %scatter_custom_fusion, s32[1024]{0:T(1024)S(1)} %bitcast.63, f32[1024,128]{1,0:T(8,128)S(1)} %copy.25), kind=kCustom, calls=%fused_computation.4 | custom fusion | flops 131072 | bytes 1576960 | tf_op jit(solution)/shard_map/scatter-add | solution.py:225
  55.5 1.3 slice.28.refs_0_
  56.8 17.6 %shard_map.167 = (bf16[256,128]{1,0:T(8,128)(2,1)}, bf16[2048,128]{1,0:T(8,128)(2,1)S(1)}) custom-call(bf16[2048,128]{1,0:T(8,128)(2,1)S(1)} %slice.28.refs_0_, bf16[256,128]{1,0:T(8,128)(2,1)S(1)} %copy-done.1), custom_call_target="tpu_custom_call" | custom-call | tf_op jit(solution)/shard_map/pallas_call | solution.py:163
  74.4 0.5 compare_and_fusion.2
  75.0 1.7 convolution_convert_fusion.5
  76.7 1.8 convolution_bitcast_fusion
  78.5 14.2 %scatter_fusion.1 = f32[7168,128]{1,0:T(8,128)} fusion(f32[7168,128]{1,0:T(8,128)} %scatter_fusion, s32[2048]{0:T(1024)S(1)} %bitcast.61, f32[2048,128]{1,0:T(8,128)S(1)} %convolution_bitcast_fusion), kind=kCustom, calls=%fused_computation.5 | custom fusion | flops 262144 | bytes 3153920 | tf_op jit(solution)/shard_map/scatter-add | solution.py:225
  92.7 1.7 slice.27.refs_0_
  94.4 31.1 %shard_map.168 = (bf16[256,128]{1,0:T(8,128)(2,1)}, bf16[4096,128]{1,0:T(8,128)(2,1)S(1)}) custom-call(bf16[4096,128]{1,0:T(8,128)(2,1)S(1)} %slice.27.refs_0_, bf16[256,128]{1,0:T(8,128)(2,1)S(1)} %copy-done.2), custom_call_target="tpu_custom_call" | custom-call | tf_op jit(solution)/shard_map/pallas_call | solution.py:163
  125.5 4.7 %fusion.refs_0_ = bf16[4096,128]{1,0:T(8,128)(2,1)S(1)} fusion(bf16[256,4096]{1,0:T(8,128)(2,1)} %all-gather.8.cloned.1.call-done, bf16[4096,128]{1,0:T(8,128)(2,1)S(1)} %get-tuple-element.17), kind=kOutput, calls=%fused_computation.7 | convolution fusion | flops 537427968 | bytes 4194304 | tf_op jit(solution)/shard_map/dot_general | solution.py:176
  130.2 28.4 %shard_map.169 = (bf16[256,128]{1,0:T(8,128)(2,1)S(1)}, bf16[4096,128]{1,0:T(8,128)(2,1)S(1)}) custom-call(bf16[4096,128]{1,0:T(8,128)(2,1)S(1)} %fusion.refs_0_), custom_call_target="tpu_custom_call" | custom-call | tf_op jit(solution)/shard_map/pallas_call | solution.py:163
  158.6 6.2 %gather_fusion = bf16[2048,128]{1,0:T(8,128)(2,1)S(1)} fusion(bf16[4096,128]{1,0:T(8,128)(2,1)S(1)} %get-tuple-element.19, s32[2048]{0:T(1024)S(1)} %broadcast_clamp_fusion), kind=kCustom, calls=%fused_computation | custom fusion | bytes 1056768 | tf_op jit(solution)/shard_map/jit(_take)/gather | solution.py:232
  164.8 2.9 %fusion.1.refs_0_ = bf16[2048,128]{1,0:T(8,128)(2,1)S(1)} fusion(bf16[256,2048]{1,0:T(8,128)(2,1)S(1)} %copy-done.6, bf16[256,2048]{1,0:T(8,128)(2,1)} %all-gather.6.cloned.1.call-done, bf16[2048,128]{1,0:T(8,128)(2,1)S(1)} %gather_fusion, pred[2048]{0:T(1024)(128)(4,1)S(1)} %compare_and_fusion, bf16[128,256]{1,0:T(8,128)(2,1)S(1)} %convolution_convert_fusion.5), kind=kOutput, calls=%fused_computation.10 | convolution fusion | flops 269058048 | bytes 3213312 | tf_op jit(solution)/shard_map/dot_general | solution.py:176
  167.8 17.2 %shard_map.170 = (bf16[256,128]{1,0:T(8,128)(2,1)S(1)}, bf16[2048,128]{1,0:T(8,128)(2,1)S(1)}) custom-call(bf16[2048,128]{1,0:T(8,128)(2,1)S(1)} %fusion.1.refs_0_), custom_call_target="tpu_custom_call" | custom-call | tf_op jit(solution)/shard_map/pallas_call | solution.py:163
  185.0 0.1 pad_maximum_fusion.1
  185.1 4.3 %gather_fusion.1 = bf16[1024,128]{1,0:T(8,128)(2,1)} fusion(bf16[6144,128]{1,0:T(8,128)(2,1)S(1)} %pad_maximum_fusion.1, s32[1024]{0:T(1024)S(1)} %broadcast_clamp_fusion.1), kind=kCustom, calls=%fused_computation.1 | custom fusion | bytes 528384 | tf_op jit(solution)/shard_map/jit(_take)/gather | solution.py:232
  189.3 2.3 %fusion.4.refs_0_ = bf16[1024,128]{1,0:T(8,128)(2,1)S(1)} fusion(bf16[256,1024]{1,0:T(8,128)(2,1)} %copy-done.4, bf16[256,1024]{1,0:T(8,128)(2,1)} %copy-done.5, bf16[1024,128]{1,0:T(8,128)(2,1)} %gather_fusion.1, pred[1024]{0:T(1024)(128)(4,1)S(1)} %compare_and_fusion.1, bf16[128,256]{1,0:T(8,128)(2,1)S(1)} %convolution_convert_fusion.6), kind=kOutput, calls=%fused_computation.18 | convolution fusion | flops 134578176 | bytes 1639424 | tf_op jit(solution)/shard_map/dot_general | solution.py:176
  191.7 9.6 %shard_map.171 = (bf16[256,128]{1,0:T(8,128)(2,1)S(1)}, bf16[1024,128]{1,0:T(8,128)(2,1)S(1)}) custom-call(bf16[1024,128]{1,0:T(8,128)(2,1)S(1)} %fusion.4.refs_0_), custom_call_target="tpu_custom_call" | custom-call | tf_op jit(solution)/shard_map/pallas_call | solution.py:163
  201.3 1.4 pad_maximum_fusion
  202.7 2.8 %gather_fusion.2 = bf16[512,128]{1,0:T(8,128)(2,1)S(1)} fusion(bf16[7168,128]{1,0:T(8,128)(2,1)} %pad_maximum_fusion, s32[1024]{0:T(1024)S(1)} %pad_clamp_fusion), kind=kCustom, calls=%fused_computation.2 | custom fusion | bytes 264192 | tf_op jit(solution)/shard_map/jit(_take)/gather | solution.py:232
  205.5 0.5 fusion.6.refs_0_
  206.0 4.3 %shard_map.172 = bf16[256,128]{1,0:T(8,128)(2,1)S(1)} custom-call(bf16[512,128]{1,0:T(8,128)(2,1)S(1)} %fusion.6.refs_0_), custom_call_target="tpu_custom_call" | custom-call | tf_op jit(solution)/shard_map/pallas_call | solution.py:163
  210.4 0.6 copy.40
  211.0 0.6 copy.41
  211.7 0.6 copy.42
  212.3 0.6 copy.43
  (41 shorter events, 0.3 us)
Async XLA Ops:
  7.2 67.8 %all-gather.4.cloned.1.call-start = ((), (), s32[]{:S(2)}) async-start(), calls=%async_computation | async-start | bytes 1572864 | tf_op jit(solution)/shard_map/all_gather | solution.py:197
  7.9 68.8 %all-gather.6.cloned.1.call-start = ((), (), s32[]{:S(2)}) async-start(), calls=%async_computation.1 | async-start | bytes 1572864 | tf_op jit(solution)/shard_map/all_gather | solution.py:197
  8.6 116.9 %all-gather.8.cloned.1.call-start = ((), (), s32[]{:S(2)}) async-start(), calls=%async_computation.2 | async-start | bytes 3145728 | tf_op jit(solution)/shard_map/all_gather | solution.py:197
  11.7 0.8 copy-start.3
  12.6 8.5 %copy-start.7 = (bf16[256,512]{1,0:T(8,128)(2,1)}, bf16[256,512]{1,0:T(8,128)(2,1)S(1)}, u32[]{:S(2)}) copy-start(bf16[256,512]{1,0:T(8,128)(2,1)S(1)} %all_gather.21) | copy-start | bytes 786436
  12.6 15.3 %copy-start.11 = (bf16[128,1024]{1,0:T(8,128)(2,1)S(1)}, bf16[128,1024]{1,0:T(8,128)(2,1)}, u32[]{:S(2)}) copy-start(bf16[128,1024]{1,0:T(8,128)(2,1)} %param.20) | copy-start | bytes 786436
  20.8 0.7 copy-start.9
  21.5 8.6 %copy-start.12 = (bf16[128,1024]{1,0:T(8,128)(2,1)S(1)}, bf16[128,1024]{1,0:T(8,128)(2,1)}, u32[]{:S(2)}) copy-start(bf16[128,1024]{1,0:T(8,128)(2,1)} %param.23) | copy-start | bytes 786436
  21.7 10.5 %copy-start = (bf16[256,128]{1,0:T(8,128)(2,1)S(1)}, bf16[256,128]{1,0:T(8,128)(2,1)}, u32[]{:S(2)}) copy-start(bf16[256,128]{1,0:T(8,128)(2,1)} %refs_1_.3) | copy-start | bytes 196612
  30.1 14.9 %copy-start.4 = (bf16[256,1024]{1,0:T(8,128)(2,1)}, bf16[256,1024]{1,0:T(8,128)(2,1)S(1)}, u32[]{:S(2)}) copy-start(bf16[256,1024]{1,0:T(8,128)(2,1)S(1)} %all_gather.23) | copy-start | bytes 1572868
  32.3 12.7 %copy-start.5 = (bf16[256,1024]{1,0:T(8,128)(2,1)}, bf16[256,1024]{1,0:T(8,128)(2,1)S(1)}, u32[]{:S(2)}) copy-start(bf16[256,1024]{1,0:T(8,128)(2,1)S(1)} %all_gather.24) | copy-start | bytes 1572868
  46.2 10.6 %copy-start.1 = (bf16[256,128]{1,0:T(8,128)(2,1)S(1)}, bf16[256,128]{1,0:T(8,128)(2,1)}, u32[]{:S(2)}) copy-start(bf16[256,128]{1,0:T(8,128)(2,1)} %refs_1_.4) | copy-start | bytes 196612
  46.2 28.7 %copy-start.13 = (s32[2,2048]{1,0:T(2,128)S(1)}, s32[2,2048]{1,0:T(2,128)}, u32[]{:S(2)}) copy-start(s32[2,2048]{1,0:T(2,128)} %param.25) | copy-start | bytes 49156
  78.5 15.9 %copy-start.2 = (bf16[256,128]{1,0:T(8,128)(2,1)S(1)}, bf16[256,128]{1,0:T(8,128)(2,1)}, u32[]{:S(2)}) copy-start(bf16[256,128]{1,0:T(8,128)(2,1)} %refs_1_.5) | copy-start | bytes 196612
  130.2 34.6 %copy-start.6 = (bf16[256,2048]{1,0:T(8,128)(2,1)S(1)}, bf16[256,2048]{1,0:T(8,128)(2,1)}, u32[]{:S(2)}) copy-start(bf16[256,2048]{1,0:T(8,128)(2,1)} %all-gather.4.cloned.1.call-done) | copy-start | bytes 3145732
  189.3 16.1 %copy-start.8 = (bf16[256,512]{1,0:T(8,128)(2,1)S(1)}, bf16[256,512]{1,0:T(8,128)(2,1)}, u32[]{:S(2)}) copy-start(bf16[256,512]{1,0:T(8,128)(2,1)} %copy-done.7) | copy-start | bytes 786436
  189.3 16.1 %copy-start.10 = (bf16[256,512]{1,0:T(8,128)(2,1)S(1)}, bf16[256,512]{1,0:T(8,128)(2,1)}, u32[]{:S(2)}) copy-start(bf16[256,512]{1,0:T(8,128)(2,1)} %copy-done.9) | copy-start | bytes 786436
  189.3 16.2 %copy-start.14 = (pred[512]{0:T(512)(128)(4,1)S(1)}, pred[512]{0:T(512)(128)(4,1)}, u32[]{:S(2)}) copy-start(pred[512]{0:T(512)(128)(4,1)} %compare_and_fusion.2) | copy-start | bytes 1540
Sparse Core Ops, SparseCore 0:
  9.5 11.8 all-gather.3
  23.0 10.2 all-gather.5
  34.8 12.0 all-gather.7

commit v2 on v0

v2 whole, which is shorter than its diff:
```python
import functools

import jax
import jax.numpy as jnp
from jax import lax
from jax.experimental import pallas as pl
from jax.experimental.pallas import tpu as pltpu
from jax.sharding import PartitionSpec as P

LEVELS = 4
MESH = pl.DeviceIdType.MESH
BF16 = jnp.bfloat16
F32 = jnp.float32


def split_group(groups):
    low, high = groups, 1
    while low > 8 or (high > 1 and low > 4 and high < 4):
        low, high = low // 2, high * 2
    return low, high


def contract_rows(left, right):
    return lax.dot_general(left, right, (((0,), (0,)), ((), ())), preferred_element_type=F32)


def kernel(leaf_count, panel_count, *refs):
    refs = list(refs)

    def take(count):
        taken = refs[:count]
        del refs[:count]
        return taken

    rhs = take(LEVELS)
    inv_in = take(LEVELS)
    coup_in = [None] + take(LEVELS - 1)
    list_rows, list_cols = take(2)
    outs = take(LEVELS)
    inv = take(LEVELS)
    coup = [None] + take(LEVELS - 1)
    forwards = take(LEVELS)
    updates, picked = take(2)
    factor_local, factor_send, factor_recv = take(3)
    levels_forward = [None] * LEVELS
    levels_backward = [None] * LEVELS
    for depth in range(LEVELS):
        levels_forward[depth] = (take(9) if depth < LEVELS - 1 else None, take(5))
        levels_backward[depth] = (take(9), take(5) if depth < LEVELS - 1 else None)

    me = lax.axis_index("leaf")
    panel = lax.axis_index("panel")
    rows, columns = rhs[0].shape
    factor_rows = inv_in[0].shape[0]
    sizes = [ref.shape[1] for ref in inv_in]
    offsets = [sum(sizes[:depth]) for depth in range(LEVELS)]
    places = [None] + [sum(sizes[1:depth]) for depth in range(1, LEVELS + 1)]
    chunk = list_rows.shape[1]
    streamed = rows % 128 == 0
    merged = factor_rows % 16 == 0

    masks = set()
    for depth in range(LEVELS):
        low, high = split_group(leaf_count >> depth)
        masks |= set(range(1, low)) | set(low * plane for plane in range(1, high))
    barrier = pltpu.get_barrier_semaphore()
    for mask in sorted(masks):
        pl.semaphore_signal(barrier, inc=1, device_id=(me ^ mask, panel), device_id_type=MESH)
    for shift in range(1, panel_count):
        pl.semaphore_signal(
            barrier, inc=1, device_id=(me, lax.rem(panel + shift, panel_count)), device_id_type=MESH
        )

    def local_factor(source, target, slot):
        return pltpu.make_async_copy(source, target.at[panel], factor_local.at[slot])

    def remote_factor(source, target, slot, shift):
        return pltpu.make_async_remote_copy(
            src_ref=source, dst_ref=target.at[panel],
            send_sem=factor_send.at[slot, shift - 1], recv_sem=factor_recv.at[slot, shift - 1],
            device_id=(me, lax.rem(panel + shift, panel_count)), device_id_type=MESH,
        )

    factors = []
    for depth in reversed(range(LEVELS)):
        factors.append((inv_in[depth], inv[depth], depth))
        if depth:
            factors.append((coup_in[depth], coup[depth], LEVELS + depth))
    for factor in factors:
        local_factor(*factor).start()
    pl.semaphore_wait(barrier, len(masks) + panel_count - 1)
    for factor in factors:
        for shift in range(1, panel_count):
            remote_factor(*factor, shift).start()

    def wait_factor(slot):
        for factor in factors:
            if factor[2] == slot:
                local_factor(*factor).wait()
                for shift in range(1, panel_count):
                    remote_factor(*factor, shift).wait_recv()

    def row_parts(ref, start, size):
        if merged:
            value = ref[:, :, pl.ds(start, size)]
            return [value.reshape(panel_count * factor_rows, size)]
        return [ref[index, :, pl.ds(start, size)] for index in range(panel_count)]

    def contracted(ref, start, size, values):
        total = None
        for index, part in enumerate(row_parts(ref, start, size)):
            term = contract_rows(part, values[index])
            total = term if total is None else total + term
        return total

    def read_values(ref):
        if merged:
            return [ref[...].reshape(panel_count * factor_rows, columns)]
        return [ref[index] for index in range(panel_count)]

    def write_values(ref, values):
        if merged:
            ref[...] = values[0].reshape(panel_count, factor_rows, columns)
        else:
            for index in range(panel_count):
                ref[index] = values[index]

    def block_of(ref, index):
        return ref.at[pl.ds(pl.multiple_of(index * rows, rows), rows)]

    def remote(source, target, send, recv, mask):
        return pltpu.make_async_remote_copy(
            src_ref=source, dst_ref=target, send_sem=send, recv_sem=recv,
            device_id=(me ^ mask, panel), device_id_type=MESH,
        )

    late = []

    def reduce_blocks(depth, buffers, block_value):
        part, kept, low_buf, high_out, high_buf, low_send, low_recv, high_send, high_recv = buffers
        groups = leaf_count >> depth
        mine = lax.rem(me, groups)
        low, high = split_group(groups)

        def low_copy(plane, step):
            return remote(
                block_of(part, mine ^ (plane * low + step)), low_buf.at[plane, step - 1],
                low_send.at[plane, step - 1], low_recv.at[plane, step - 1], step,
            )

        def issue(plane):
            def one(count, carry):
                step = low - 1 - count
                index = mine ^ (plane * low + step)
                block_of(part, index)[...] = block_value(index).astype(BF16)
                low_copy(plane, step).start()
                return carry

            lax.fori_loop(0, low - 1, one, 0)
            kept[plane] = block_value(mine ^ (plane * low))

        def high_copy(plane):
            return remote(
                high_out.at[plane - 1], high_buf.at[plane - 1],
                high_send.at[plane - 1], high_recv.at[plane - 1], plane * low,
            )

        def plane_sum(plane):
            total = kept[plane]
            for step in range(1, low):
                low_copy(plane, step).wait_recv()
                late.append(low_copy(plane, step))
                total = total + low_buf[plane, step - 1].astype(F32)
            return total

        issue(high - 1)
        for plane in range(high - 1, 0, -1):
            issue(plane - 1)
            high_out[plane - 1] = plane_sum(plane).astype(BF16)
            high_copy(plane).start()
            late.append(high_copy(plane))
        total = plane_sum(0)
        for plane in range(1, high):
            high_copy(plane).wait_recv()
            total = total + high_buf[plane - 1].astype(F32)
        return total

    def gather_blocks(depth, buffers, use):
        full, low_send, low_recv, high_send, high_recv = buffers
        groups = leaf_count >> depth
        mine = lax.rem(me, groups)
        low, high = split_group(groups)

        def low_copy(plane, step):
            here = block_of(full, mine ^ (plane * low))
            return remote(
                here, here, low_send.at[plane, step - 1], low_recv.at[plane, step - 1], step
            )

        def high_copy(plane):
            here = block_of(full, mine)
            return remote(
                here, here, high_send.at[plane - 1], high_recv.at[plane - 1], plane * low
            )

        def use_low(plane):
            for step in range(1, low):
                low_copy(plane, step).wait_recv()
                use(mine ^ (plane * low + step))

        for plane in range(high - 1, 0, -1):
            high_copy(plane).start()
            late.append(high_copy(plane))
        for plane in range(high):
            if plane:
                high_copy(plane).wait_recv()
            for step in range(low - 1, 0, -1):
                low_copy(plane, step).start()
                late.append(low_copy(plane, step))
            use(mine ^ (plane * low))
            if plane:
                use_low(plane - 1)
        use_low(high - 1)

    def aligned(start):
        return pl.multiple_of(start, rows)

    for depth in reversed(range(LEVELS)):
        groups = leaf_count >> depth
        mine = lax.rem(me, groups)
        reducing, gathering = levels_forward[depth]
        full = gathering[0]
        if reducing is not None:
            first_chunk = places[depth + 1] // chunk

            def scattered(index, depth=depth, first_chunk=first_chunk):
                base = offsets[depth] + index * rows
                row_ids = lax.broadcasted_iota(jnp.int32, (rows, chunk), 0) + base

                def one(step, total):
                    ones = jnp.where(list_rows[pl.ds(step, 1), :] == row_ids, 1.0, 0.0)
                    start = pl.multiple_of(step * chunk, chunk)
                    values = updates[pl.ds(start, chunk), :]
                    return total + jnp.dot(ones.astype(BF16), values, preferred_element_type=F32)

                return lax.fori_loop(
                    first_chunk, list_rows.shape[0], one, jnp.zeros((rows, columns), F32)
                )

            total = reduce_blocks(depth, reducing, scattered)
            combined = (total + rhs[depth][...].astype(F32)).astype(BF16)
        else:
            combined = rhs[depth][...]
        block_of(full, mine)[...] = combined
        sums = [None]
        ready = [False]

        def multiply(index, depth=depth, full=full, sums=sums, ready=ready):
            if not streamed:
                return
            if not ready[0]:
                wait_factor(depth)
                ready[0] = True
            part = row_parts(inv[depth], aligned(index * rows), rows)
            block = block_of(full, index)[...]
            terms = [jnp.dot(value, block, preferred_element_type=F32) for value in part]
            old = sums[0]
            sums[0] = terms if old is None else [a + b for a, b in zip(old, terms)]

        gather_blocks(depth, gathering, multiply)
        if not streamed:
            wait_factor(depth)
            part = row_parts(inv[depth], 0, sizes[depth])
            sums[0] = [jnp.dot(value, full[...], preferred_element_type=F32) for value in part]
        values = [value.astype(BF16) for value in sums[0]]
        write_values(forwards[depth], values)
        if depth:
            wait_factor(LEVELS + depth)

            def update_chunk(step, carry, depth=depth, values=values):
                start = pl.multiple_of(step * chunk, chunk)
                place = pl.multiple_of(places[depth] + step * chunk, chunk)
                values = read_values(forwards[depth])
                updates[pl.ds(place, chunk), :] = contracted(
                    coup[depth], start, chunk, values
                ).astype(BF16)
                return carry

            lax.fori_loop(0, sizes[depth] // chunk, update_chunk, 0)

    picked[...] = jnp.zeros_like(picked)
    for depth in range(LEVELS):
        groups = leaf_count >> depth
        mine = lax.rem(me, groups)
        reducing, gathering = levels_backward[depth]
        if depth:
            def pull(step, totals, depth=depth):
                start = pl.multiple_of(step * chunk, chunk)
                place = pl.multiple_of(places[depth] + step * chunk, chunk)
                part = row_parts(coup[depth], start, chunk)
                rows_now = picked[pl.ds(place, chunk), :].astype(BF16)
                return [
                    total - jnp.dot(value, rows_now, preferred_element_type=F32)
                    for total, value in zip(totals, part)
                ]

            totals = [value.astype(F32) for value in read_values(forwards[depth])]
            totals = lax.fori_loop(0, sizes[depth] // chunk, pull, totals)
            write_values(forwards[depth], [value.astype(BF16) for value in totals])

        if streamed:
            def product(index, depth=depth):
                values = read_values(forwards[depth])
                return contracted(inv[depth], aligned(index * rows), rows, values)
        else:
            whole_product = reducing[0]
            values = read_values(forwards[depth])
            whole_product[...] = contracted(inv[depth], 0, sizes[depth], values).astype(BF16)

            def product(index, whole_product=whole_product):
                return block_of(whole_product, index)[...].astype(F32)

        solved = reduce_blocks(depth, reducing, product).astype(BF16)
        outs[depth][...] = solved
        if gathering is not None:
            full = gathering[0]
            block_of(full, mine)[...] = solved
            first_chunk = places[depth + 1] // chunk

            def pick(index, depth=depth, full=full, first_chunk=first_chunk):
                base = offsets[depth] + index * rows
                row_ids = lax.broadcasted_iota(jnp.int32, (chunk, rows), 1) + base
                block = block_of(full, index)[...]

                def one(step, carry):
                    start = pl.multiple_of(step * chunk, chunk)
                    here = pl.ds(start, chunk)
                    ones = jnp.where(list_cols[here, :] == row_ids, 1.0, 0.0).astype(BF16)
                    picked[here, :] += jnp.dot(ones, block, preferred_element_type=F32)
                    return carry

                lax.fori_loop(first_chunk, list_rows.shape[0], one, 0)

            gather_blocks(depth, gathering, pick)

    for copy in late:
        copy.wait_send()
    for factor in factors:
        for shift in range(1, panel_count):
            remote_factor(*factor, shift).wait_send()


def body(*args):
    rhs, inv, coup, lists = args[:4], args[4:8], args[8:11], args[11:]
    rows, columns = rhs[0].shape
    leaf_count = lax.axis_size("leaf")
    panel_count = lax.axis_size("panel")
    factor_rows = inv[0].shape[0]
    sizes = [value.shape[1] for value in inv]
    chunk = sizes[-1]
    leaf = lax.axis_index("leaf")
    chosen = []
    for depth in range(1, LEVELS):
        front = leaf // (leaf_count >> depth)
        chosen.append(lax.dynamic_index_in_dim(lists[depth - 1], front, 0, keepdims=False))
    joined = jnp.concatenate(chosen)
    list_rows = joined.reshape(-1, chunk)
    list_cols = joined.reshape(-1, 1)
    dma = pltpu.SemaphoreType.DMA
    vmem = pltpu.VMEM
    scratch = [vmem((panel_count, factor_rows, size), BF16) for size in sizes]
    scratch += [vmem((panel_count, factor_rows, size), BF16) for size in sizes[1:]]
    scratch += [vmem((panel_count, factor_rows, columns), BF16) for _ in sizes]
    scratch += [vmem((joined.shape[0], columns), BF16), vmem((joined.shape[0], columns), F32)]
    peers = max(panel_count - 1, 1)
    scratch += [dma((2 * LEVELS,)), dma((2 * LEVELS, peers)), dma((2 * LEVELS, peers))]

    def reduce_scratch(depth):
        low, high = split_group(leaf_count >> depth)
        highs = max(high - 1, 1)
        lows = max(low - 1, 1)
        return [
            vmem((sizes[depth], columns), BF16),
            vmem((high, rows, columns), F32),
            vmem((high, lows, rows, columns), BF16),
            vmem((highs, rows, columns), BF16),
            vmem((highs, rows, columns), BF16),
            dma((high, lows)), dma((high, lows)), dma((highs,)), dma((highs,)),
        ]

    def gather_scratch(depth):
        low, high = split_group(leaf_count >> depth)
        highs = max(high - 1, 1)
        lows = max(low - 1, 1)
        return [
            vmem((sizes[depth], columns), BF16),
            dma((high, lows)), dma((high, lows)), dma((highs,)), dma((highs,)),
        ]

    for depth in range(LEVELS):
        if depth < LEVELS - 1:
            scratch += reduce_scratch(depth)
        scratch += gather_scratch(depth)
        scratch += reduce_scratch(depth)
        if depth < LEVELS - 1:
            scratch += gather_scratch(depth)

    in_vmem = pl.BlockSpec(memory_space=vmem)
    anywhere = pl.BlockSpec(memory_space=pl.ANY)
    own = jax.ShapeDtypeStruct((rows, columns), BF16)
    return pl.pallas_call(
        functools.partial(kernel, leaf_count, panel_count),
        out_shape=(own,) * LEVELS,
        in_specs=[in_vmem] * LEVELS + [anywhere] * (2 * LEVELS - 1) + [in_vmem] * 2,
        out_specs=(in_vmem,) * LEVELS,
        scratch_shapes=scratch,
        compiler_params=pltpu.CompilerParams(
            collective_id=0, has_side_effects=True, vmem_limit_bytes=48 * 2**20
        ),
    )(*rhs, *inv, *coup, list_rows, list_cols)


def solution(mesh):
    in_specs = (P("leaf", "panel"),) * 4 + (P(("leaf", "panel"), None),) * 7 + (P(),) * 3
    out_specs = (P("leaf", "panel"),) * 4
    return jax.shard_map(body, mesh=mesh, in_specs=in_specs, out_specs=out_specs, check_vma=False)
```

time: 581 us -> 177 us (0.30)
  waiting for transfers between devices: 438 us -> 0 us
  Pallas kernels: 0 us -> 164 us
  other arithmetic: 35.6 us -> 0.01 us
  starting transfers between devices: 31.9 us -> 0 us
  local copies, waits for them, and re-layouts: 36.7 us -> 10.1 us
  matrix products: 14 us -> 0 us
  between operations: 14.8 us -> 0.82 us
  blocking collectives: 8.72 us -> 0 us
    all_gather x7 -> x0, waiting for transfers between devices: 229 us -> none  [the longest x4 221 us: collect_rows(): gathered = lax.all_gather(own_block, 'leaf', axis=0, tiled=True)]
    ppermute x24 -> x0, waiting for transfers between devices: 208 us -> none  [swapped(): return lax.ppermute(value, axis, pairs)]
    pallas_call x0 -> x1, Pallas kernels: none -> 164 us  [body(): pl.pallas_call(functools.partial(kernel, leaf_count, panel_count), out_sh...]
    ppermute x24 -> x0, starting transfers between devices: 31.4 us -> none  [swapped(): return lax.ppermute(value, axis, pairs)]
    scatter-add x3 -> x0, other arithmetic: 27.6 us -> none  [body(): accumulated = accumulated.at[row_list].add(update)]
    gather x3 -> x0, local copies, waits for them, and re-layouts: 16.9 us -> none  [body(): picked = jnp.take(anc_values, row_list, axis=0)]
    dot_general x10 -> x0, matrix products: 14 us -> none  [the longest x7 11.6 us: contract_rows(): lax.dot_general(left, right, (((0,), (0,)), ((), ())), preferred_element_...]
    scatter x5 -> x0, local copies, waits for them, and re-layouts: 9.44 us -> none  [body(): anc_values.at[offsets[depth_now]:offsets[depth_now] + front_rows]]
  transfers between devices with their start and end apart: 31 -> 0, of which waited for: 28 -> 0; matrix products, arithmetic and copies ran while one was open for 2% -> 0% of each run, Pallas kernels for 0% -> 0%
where the time goes in v2:
time: 177 us; the launch traced here: 175 us
  Pallas kernels  164 us (93%)
  local copies, waits for them, and re-layouts  10.1 us (6%)
    pallas_call x1, Pallas kernels, body(): pl.pallas_call(functools.partial(kernel, leaf_count, panel_count), out_sh...  164 us
    unnamed x28, local copies, waits for them, and re-layouts  7.96 us

profile of v2, /device:TPU:0, one launch (start us, length us, event | category | flops | bytes accessed | tf_op | source)
XLA Modules:
  0.0 175.2 jit_solution(16193463209350154092)
XLA Ops:
  0.6 0.0 copy-start
  0.6 0.0 copy-start.6
  0.7 0.0 copy-start.4
  0.7 0.0 copy-start.2
  0.7 0.0 copy-start.1
  0.7 0.0 copy-start.8
  0.7 0.9 constant_dynamic-slice_fusion
  1.6 0.7 constant_dynamic-slice_fusion.1
  2.3 0.0 copy-done
  2.4 0.5 reshape.16.refs_12_
  2.9 0.0 copy-done.6
  2.9 0.0 copy-done.4
  2.9 0.0 copy-done.2
  2.9 0.0 copy-done.1
  3.0 0.0 copy-done.8
  3.0 0.0 copy-start.3
  3.0 1.0 copy-done.3
  4.0 0.0 copy-start.5
  4.0 0.9 copy-done.5
  5.0 0.0 copy-start.7
  5.0 0.9 copy-done.7
  5.9 0.0 copy-start.9
  5.9 0.8 copy-done.9
  6.7 0.0 copy-start.10
  6.7 0.8 copy-done.10
  7.5 0.0 copy-start.11
  7.5 0.8 copy-done.11
  8.4 164.3 %shard_map.165 = (bf16[256,128]{1,0:T(8,128)(2,1)S(1)}, bf16[256,128]{1,0:T(8,128)(2,1)S(1)}, bf16[256,128]{1,0:T(8,128)(2,1)S(1)}, bf16[256,128]{1,0:T(8,128)(2,1)S(1)}) custom-call(bf16[256,128]{1,0:T(8,128)(2,1)S(1)} %copy-done.8, bf16[256,128]{1,0:T(8,128)(2,1)S(1)} %copy-done.9, bf16[256,128]{1,0:T(8,128)(2,1)S(1)} %copy-done.10, ...), custom_call_target="tpu_custom_call" | custom-call | tf_op jit(solution)/shard_map/pallas_call | solution.py:411
  172.7 0.6 copy.23
  173.4 0.6 copy.24
  174.0 0.6 copy.25
  174.6 0.6 copy.26
  (3 shorter events, 0.0 us)
Async XLA Ops:
  0.6 1.7 copy-start
  0.6 2.3 %copy-start.6 = (bf16[128,512]{1,0:T(8,128)(2,1)S(1)}, bf16[128,512]{1,0:T(8,128)(2,1)}, u32[]{:S(2)}) copy-start(bf16[128,512]{1,0:T(8,128)(2,1)} %refs_7_.1) | copy-start | bytes 393220
  0.7 2.3 %copy-start.4 = (bf16[128,1024]{1,0:T(8,128)(2,1)S(1)}, bf16[128,1024]{1,0:T(8,128)(2,1)}, u32[]{:S(2)}) copy-start(bf16[128,1024]{1,0:T(8,128)(2,1)} %refs_6_.1) | copy-start | bytes 786436
  0.7 2.3 %copy-start.2 = (bf16[128,2048]{1,0:T(8,128)(2,1)S(1)}, bf16[128,2048]{1,0:T(8,128)(2,1)}, u32[]{:S(2)}) copy-start(bf16[128,2048]{1,0:T(8,128)(2,1)} %refs_5_.1) | copy-start | bytes 1572868
  0.7 2.3 %copy-start.1 = (bf16[128,4096]{1,0:T(8,128)(2,1)S(1)}, bf16[128,4096]{1,0:T(8,128)(2,1)}, u32[]{:S(2)}) copy-start(bf16[128,4096]{1,0:T(8,128)(2,1)} %refs_4_.1) | copy-start | bytes 3145732
  0.7 2.3 %copy-start.8 = (bf16[256,128]{1,0:T(8,128)(2,1)S(1)}, bf16[256,128]{1,0:T(8,128)(2,1)}, u32[]{:S(2)}) copy-start(bf16[256,128]{1,0:T(8,128)(2,1)} %refs_0_.1) | copy-start | bytes 196612
  3.0 1.0 copy-start.3
  4.0 0.9 copy-start.5
  5.0 0.9 copy-start.7
  5.9 0.8 copy-start.9
  6.7 0.8 copy-start.10
  7.5 0.8 copy-start.11

commit v3 on v2

--- a/solution.py
+++ b/solution.py
@@ -244,7 +244,8 @@
                     return total + jnp.dot(ones.astype(BF16), values, preferred_element_type=F32)
 
                 return lax.fori_loop(
-                    first_chunk, list_rows.shape[0], one, jnp.zeros((rows, columns), F32)
+                    first_chunk, list_rows.shape[0], one, jnp.zeros((rows, columns), F32),
+                    unroll=True,
                 )
 
             total = reduce_blocks(depth, reducing, scattered)
@@ -286,7 +287,7 @@
                 ).astype(BF16)
                 return carry
 
-            lax.fori_loop(0, sizes[depth] // chunk, update_chunk, 0)
+            lax.fori_loop(0, sizes[depth] // chunk, update_chunk, 0, unroll=True)
 
     picked[...] = jnp.zeros_like(picked)
     for depth in range(LEVELS):
@@ -305,7 +306,7 @@
                 ]
 
             totals = [value.astype(F32) for value in read_values(forwards[depth])]
-            totals = lax.fori_loop(0, sizes[depth] // chunk, pull, totals)
+            totals = lax.fori_loop(0, sizes[depth] // chunk, pull, totals, unroll=True)
             write_values(forwards[depth], [value.astype(BF16) for value in totals])
 
         if streamed:
@@ -339,7 +340,7 @@
                     picked[here, :] += jnp.dot(ones, block, preferred_element_type=F32)
                     return carry
 
-                lax.fori_loop(first_chunk, list_rows.shape[0], one, 0)
+                lax.fori_loop(first_chunk, list_rows.shape[0], one, 0, unroll=True)
 
             gather_blocks(depth, gathering, pick)
 
@@ -406,7 +407,7 @@
             scratch += gather_scratch(depth)
 
     in_vmem = pl.BlockSpec(memory_space=vmem)
-    anywhere = pl.BlockSpec(memory_space=pl.ANY)
+    anywhere = pl.BlockSpec(memory_space=pltpu.HBM)
     own = jax.ShapeDtypeStruct((rows, columns), BF16)
     return pl.pallas_call(
         functools.partial(kernel, leaf_count, panel_count),

time: 177 us -> 146 us (0.82)
  Pallas kernels: 164 us -> 134 us
    pallas_call x1, Pallas kernels: 164 us -> 134 us  [body(): pl.pallas_call(functools.partial(kernel, leaf_count, panel_count), out_sh...]
where the time goes in v3:
time: 146 us; the launch traced here: 145 us
  Pallas kernels  134 us (92%)
  local copies, waits for them, and re-layouts  10.1 us (7%)
    pallas_call x1, Pallas kernels, body(): pl.pallas_call(functools.partial(kernel, leaf_count, panel_count), out_sh...  134 us
    unnamed x28, local copies, waits for them, and re-layouts  7.96 us

profile of v3, /device:TPU:0, one launch (start us, length us, event | category | flops | bytes accessed | tf_op | source)
XLA Modules:
  0.0 145.3 jit_solution(18339991807367988194)
XLA Ops:
  0.6 0.0 copy-start
  0.6 0.0 copy-start.6
  0.7 0.0 copy-start.4
  0.7 0.0 copy-start.2
  0.7 0.0 copy-start.1
  0.7 0.0 copy-start.8
  0.7 0.9 constant_dynamic-slice_fusion
  1.6 0.7 constant_dynamic-slice_fusion.1
  2.3 0.0 copy-done
  2.4 0.5 reshape.16.refs_12_
  2.9 0.0 copy-done.6
  2.9 0.0 copy-done.4
  2.9 0.0 copy-done.2
  2.9 0.0 copy-done.1
  3.0 0.0 copy-done.8
  3.0 0.0 copy-start.3
  3.0 1.0 copy-done.3
  4.0 0.0 copy-start.5
  4.0 0.9 copy-done.5
  5.0 0.0 copy-start.7
  5.0 0.9 copy-done.7
  5.9 0.0 copy-start.9
  5.9 0.8 copy-done.9
  6.7 0.0 copy-start.10
  6.7 0.8 copy-done.10
  7.5 0.0 copy-start.11
  7.5 0.8 copy-done.11
  8.4 134.4 %shard_map.165 = (bf16[256,128]{1,0:T(8,128)(2,1)S(1)}, bf16[256,128]{1,0:T(8,128)(2,1)S(1)}, bf16[256,128]{1,0:T(8,128)(2,1)S(1)}, bf16[256,128]{1,0:T(8,128)(2,1)S(1)}) custom-call(bf16[256,128]{1,0:T(8,128)(2,1)S(1)} %copy-done.8, bf16[256,128]{1,0:T(8,128)(2,1)S(1)} %copy-done.9, bf16[256,128]{1,0:T(8,128)(2,1)S(1)} %copy-done.10, ...), custom_call_target="tpu_custom_call" | custom-call | tf_op jit(solution)/shard_map/pallas_call | solution.py:412
  142.8 0.6 copy.23
  143.4 0.6 copy.24
  144.1 0.6 copy.25
  144.7 0.6 copy.26
  (3 shorter events, 0.0 us)
Async XLA Ops:
  0.6 1.7 %copy-start = (s32[2,2048]{1,0:T(2,128)S(1)}, s32[2,2048]{1,0:T(2,128)}, u32[]{:S(2)}) copy-start(s32[2,2048]{1,0:T(2,128)} %param.25) | copy-start | bytes 49156
  0.6 2.3 %copy-start.6 = (bf16[128,512]{1,0:T(8,128)(2,1)S(1)}, bf16[128,512]{1,0:T(8,128)(2,1)}, u32[]{:S(2)}) copy-start(bf16[128,512]{1,0:T(8,128)(2,1)} %refs_7_.1) | copy-start | bytes 393220
  0.7 2.3 %copy-start.4 = (bf16[128,1024]{1,0:T(8,128)(2,1)S(1)}, bf16[128,1024]{1,0:T(8,128)(2,1)}, u32[]{:S(2)}) copy-start(bf16[128,1024]{1,0:T(8,128)(2,1)} %refs_6_.1) | copy-start | bytes 786436
  0.7 2.3 %copy-start.2 = (bf16[128,2048]{1,0:T(8,128)(2,1)S(1)}, bf16[128,2048]{1,0:T(8,128)(2,1)}, u32[]{:S(2)}) copy-start(bf16[128,2048]{1,0:T(8,128)(2,1)} %refs_5_.1) | copy-start | bytes 1572868
  0.7 2.3 %copy-start.1 = (bf16[128,4096]{1,0:T(8,128)(2,1)S(1)}, bf16[128,4096]{1,0:T(8,128)(2,1)}, u32[]{:S(2)}) copy-start(bf16[128,4096]{1,0:T(8,128)(2,1)} %refs_4_.1) | copy-start | bytes 3145732
  0.7 2.3 %copy-start.8 = (bf16[256,128]{1,0:T(8,128)(2,1)S(1)}, bf16[256,128]{1,0:T(8,128)(2,1)}, u32[]{:S(2)}) copy-start(bf16[256,128]{1,0:T(8,128)(2,1)} %refs_0_.1) | copy-start | bytes 196612
  3.0 1.0 copy-start.3
  4.0 0.9 copy-start.5
  5.0 0.9 copy-start.7
  5.9 0.8 copy-start.9
  6.7 0.8 copy-start.10
  7.5 0.8 copy-start.11
